TPU v7x, 32 devices: a whole 2x2x4 slice. The times are simulated.
32 devices in a mesh: shots: 2 (over y), lat: 4 (over z), depth: 4 (over x, core).
Axes of the slice: x: 2, y: 2, z: 4, core: 2. Of those that a mesh axis runs over, the one named last changes fastest.
Arguments:
- source: float32 [8, 32, 1024], P('shots', 'lat'), parts along dimension 0, may hold values from -6 to 6
- traces: float32 [64, 4096], P(('shots', 'lat')), parts along dimension 0, may hold values from -6 to 6
- trace_tiles: int32 [64, 1], P(('shots', 'lat')), parts along dimension 0, may hold values from 0 to 3; in each aligned block of 8 rows (0 to 7, 8 to 15, ...) at most 5 rows name the same one
- trace_offsets: int32 [64], P(('shots', 'lat')), parts along dimension 0, may hold values from 0 to 7
- stencil: float32 [4, 2, 9, 9], replicated, may hold values from -0.9 to 0.9
- angular_freq: float32 [4], replicated, may hold values from 2 to 6
- slowness: float32 [4, 16384], P('depth', 'lat'), may hold values from 0.5 to 2
- reflect: float32 [4, 16384], P('depth', 'lat'), may hold values from -4 to 4
Outputs:
- picture: float32 [8, 16384], P(('shots', 'depth'), 'lat'), parts along dimension 0
- residual: float32 [64, 4, 1024], P(('shots', 'lat', 'depth')), parts along dimension 0
There are 2 independent parts, one for each index of `shots`. A program takes and returns all parts, laid end to end along the dimension named above; an argument that names none is the same for every part. Nothing has to cross between parts.
Inputs may be any that keep to these rules, and one draw needn't show every extreme that they name: `trace_tiles`: among the 8 blocks of one device, at most 5 name the same tile; on some device one tile is named by exactly 5 of them.
All inputs are finite; a program needn't handle non-finite values.
Results may differ from a plain program's by a relative error of at most 0.00029.
Values sent between devices are 32-bit elements; how exact they have to be, the bound alone decides.
A program may use at most 64 MiB of HBM per device.

v0:
```python
import jax
import jax.numpy as jnp
from jax import lax
from jax.sharding import PartitionSpec as P

precision_high = lax.Precision.HIGHEST


def padded_2(array, sides, width):
    for axis, dim in sides:
        count, length = (lax.axis_size(axis), array.shape[dim])
        up = [(i, (i + 1) % count) for i in range(count - 1)]
        down = [(j, i) for i, j in up]
        last = lax.slice_in_dim(array, length - width, length, axis=dim)
        leading = lax.slice_in_dim(array, 0, width, axis=dim)
        before = lax.ppermute(last, axis, up)
        after = lax.ppermute(leading, axis, down)
        array = jnp.concatenate([before, array, after], axis=dim)
    return array


def from_behind(value, axis, steps):
    count = lax.axis_size(axis)
    leading, last = (max(0, -steps), min(count, count - steps))
    return lax.ppermute(value, axis, [(source, source + steps) for source in range(leading, last)])


def broadcast(block, axis, holder):
    block = jnp.where(lax.axis_index(axis) == holder, block, jnp.zeros_like(block))
    return lax.psum(block, axis)


def make_taps(stencil):
    adjoint = jnp.stack([stencil[:, 0, ::-1, ::-1], -stencil[:, 1, ::-1, ::-1]], axis=1)
    return (stencil, adjoint)


def rotate(wave_field, phase_angle, direction):
    half_width = phase_angle.shape[-1]
    cosine = jnp.cos(phase_angle)
    sine_part = direction * jnp.sin(phase_angle)
    real_part = wave_field[..., :half_width]
    imag_part = wave_field[..., half_width:]
    return jnp.concatenate(
        [real_part * cosine - imag_part * sine_part, real_part * sine_part + imag_part * cosine],
        axis=-1,
    )


def convolve(wave_field, taps):
    tap_count = taps.shape[-1]
    tap_reach = tap_count // 2
    line_count = wave_field.shape[2]
    half_width = wave_field.shape[3] // 2
    padded = padded_2(wave_field, (("lat", 2),), tap_reach)
    widths = ((0, 0), (0, 0), (0, 0), (tap_reach, tap_reach))
    real_pad = jnp.pad(padded[..., :half_width], widths)
    imag_pad = jnp.pad(padded[..., half_width:], widths)
    out_shape = (wave_field.shape[0], wave_field.shape[1], line_count, half_width)
    out_real = jnp.zeros(out_shape, jnp.float32)
    out_imag = jnp.zeros(out_shape, jnp.float32)
    for row_tap in range(tap_count):
        for col_tap in range(tap_count):
            real_piece = real_pad[
                :, :, row_tap : row_tap + line_count, col_tap : col_tap + half_width
            ]
            imag_piece = imag_pad[
                :, :, row_tap : row_tap + line_count, col_tap : col_tap + half_width
            ]
            tap_real = taps[:, 0, row_tap, col_tap][None, :, None, None]
            tap_imag = taps[:, 1, row_tap, col_tap][None, :, None, None]
            out_real = out_real + tap_real * real_piece - tap_imag * imag_piece
            out_imag = out_imag + tap_imag * real_piece + tap_real * imag_piece
    return jnp.concatenate([out_real, out_imag], axis=-1)


def march_down(wave_field, op_table, angles):
    wave_field = rotate(convolve(wave_field, op_table), angles[0], 1.0)
    stored = [wave_field]
    return jnp.stack(stored)


def march_up(up_wave, op_table, angles, src_levels, model_pair):
    for step_index in reversed(range(angles.shape[0])):
        up_wave = up_wave + model_pair[step_index][None, None] * src_levels[step_index][None]
        up_wave = convolve(rotate(up_wave, angles[step_index], -1.0), op_table)
    return up_wave


def local(source, traces, trace_tiles, trace_offsets, stencil, angular_freq, slowness, reflect):
    freq_count, tile_rows, full_width = source.shape
    half_width = full_width // 2
    step_count = slowness.shape[0]
    depth_count = lax.axis_size("depth")
    depth_index = lax.axis_index("depth")
    forward, adjoint = make_taps(stencil)
    places = jnp.arange(tile_rows).astype(jnp.float32)
    targets = (trace_tiles[:, 0] * tile_rows + trace_offsets).astype(jnp.float32)
    lat_start = (lax.axis_index("lat") * tile_rows).astype(jnp.float32)
    piece_traces = lax.all_gather(traces, "lat", axis=0, tiled=True)
    piece_rows = lax.all_gather(targets, "lat", axis=0, tiled=True)
    selector = ((piece_rows - lat_start)[None, :] == places[:, None]).astype(jnp.float32)
    observed = jnp.dot(selector, piece_traces, precision=precision_high)
    observed = observed.reshape(tile_rows, freq_count, full_width)
    surface = jnp.transpose(observed, (1, 0, 2))
    receiver = jnp.concatenate([surface[..., :half_width], -surface[..., half_width:]], axis=-1)
    pair_fields = jnp.stack([source, receiver])
    level_slow = slowness.reshape(step_count, tile_rows, half_width)
    angles = angular_freq[None, :, None, None] * level_slow[:, None]
    model_half = reflect.reshape(step_count, tile_rows, half_width)
    model_pair = jnp.concatenate([model_half, model_half], axis=-1)
    top_slab = depth_index == 0
    top_input = jnp.where(top_slab, pair_fields, 0.0)

    def round_down(turn_index, current):
        bottom = march_down(current, forward, angles)[-1]
        return from_behind(bottom, "depth", 1) + top_input

    current = lax.fori_loop(0, depth_count - 1, round_down, top_input)
    levels = march_down(current, forward, angles)
    sources = levels[:, 0]

    def round_up(turn_index, current):
        top_field = march_up(current, adjoint, angles, sources, model_pair)
        return from_behind(top_field, "depth", -1)

    below = jnp.zeros((1, freq_count, tile_rows, full_width), jnp.float32)
    current = lax.fori_loop(0, depth_count - 1, round_up, below)
    upward = march_up(current, adjoint, angles, sources, model_pair)
    product = levels[:, 0] * levels[:, 1]
    picture = jnp.sum(product[..., :half_width] - product[..., half_width:], axis=1).reshape(
        step_count, tile_rows * half_width
    )
    surface_up = broadcast(upward[0], "depth", 0)
    row_share = tile_rows // depth_count
    row_start = depth_index * row_share
    own_part = lax.dynamic_slice_in_dim(surface_up, row_start, row_share, 1)
    own_seen = lax.dynamic_slice_in_dim(observed, row_start, row_share, 0)
    residual = jnp.transpose(own_part, (1, 0, 2)) - own_seen
    return (picture, residual)


def solution(mesh):
    in_specs = (
        P("shots", "lat", None),
        P(("shots", "lat"), None),
        P(("shots", "lat"), None),
        P(("shots", "lat")),
        P(),
        P(),
        P("depth", "lat"),
        P("depth", "lat"),
    )
    out_specs = (P(("shots", "depth"), "lat"), P(("shots", "lat", "depth"), None, None))
    return jax.shard_map(local, mesh=mesh, in_specs=in_specs, out_specs=out_specs, check_vma=False)
```

profile of v0, /device:TPU:0, one launch (start us, length us, event | category | flops | bytes accessed | tf_op | source)
XLA Modules:
  0.0 301.9 jit_solution(15912066643965686476)
XLA Ops:
  9.9 13.5 %all-reduce.8 = f32[32]{0:T(128)S(1)} all-reduce(f32[32]{0:T(128)S(1)} %fusion.48), channel_id=1, replica_groups=mesh['shots'=2,'lat'=4,'depth'=4] {'lat'}, use_global_device_ids=true, to_apply=%add.8 | all-reduce | flops 32 | bytes 256
  23.4 15.0 %all_gather.7 = f32[32,4096]{1,0:T(8,128)S(1)} all-gather(f32[8,4096]{1,0:T(8,128)} %param.13), channel_id=1, replica_groups=mesh['shots'=2,'lat'=4,'depth'=4] {'lat'}, dimensions={0}, use_global_device_ids=true | all-gather | bytes 655360 | tf_op jit(solution)/shard_map/all_gather | solution.py:100
  41.7 100.5 %while.28 = (s32[]{:T(128)}, f32[2,4,8,1024]{3,2,1,0:T(8,128)S(1)}, f32[4,2,9,9]{0,3,2,1:T(8,128)S(1)}, f32[2,4,8,1024]{3,2,1,0:T(8,128)S(1)}, f32[8,512]{1,0:T(8,128)S(1)}, /*index=5*/f32[4]{0:T(128)S(1)}, s32[]{:T(128)}) while((s32[]{:T(128)}, f32[2,4,8,1024]{3,2,1,0:T(8,128)S(1)}, f32[4,2,9,9]{0,3,2,1:T(8,128)S(1)}, ...), condition=%wide.region_1.2_spmd.clone.clone, body=%wide.region_0.1_spmd.clone.clone.sunk | while | flops 22265856 | bytes 10328341 | solution.py:119
  43.1 4.6 %collective-permute-start.1 = (f32[2,4,4,1024]{3,2,1,0:T(4,128)S(1)}, f32[2,4,4,1024]{3,2,1,0:T(4,128)S(1)}, u32[]{:S(2)}, u32[]{:S(2)}) collective-permute-start(f32[2,4,4,1024]{3,2,1,0:T(4,128)S(1)} %get-tuple-element.1461), channel_id=1, source_target_pairs={{0,4},{4,8},{8,12},{1,5},{5,9},{9,13},{2,6},{6,10},{10,14},{3,7},{... | collective-permute-start | bytes 393224 | tf_op jit(solution)/shard_map/while/body/eval_jaxpr/ppermute | solution.py:16
  50.3 18.9 %multiply_subtract_fusion.10 = (f32[2,4,8,512]{3,2,1,0:T(8,128)S(1)}, f32[2,4,8,512]{3,2,1,0:T(8,128)S(1)}, f32[2,4,8,512]{3,2,1,0:T(8,128)S(1)}) fusion(f32[4,8,512]{2,1,0:T(8,128)S(1)} %get-tuple-element.1360, f32[4,8,512]{2,1,0:T(8,128)S(1)} %get-tuple-element.1361, f32[4]{0:T(128)S(1)} %get-tuple-element.1362, f32[4]{0:T(128)S(1)} %get-tuple-element.1363, ...), kind=kLoop, calls=%fused_computation.173.clone.1 | loop fusion | flops 21757952 | bytes 2835456 | tf_op jit(solution)/shard_map/while/body/eval_jaxpr/sub | solution.py:45
  73.2 5.0 %collective-permute-start.1 = (f32[2,4,4,1024]{3,2,1,0:T(4,128)S(1)}, f32[2,4,4,1024]{3,2,1,0:T(4,128)S(1)}, u32[]{:S(2)}, u32[]{:S(2)}) collective-permute-start(f32[2,4,4,1024]{3,2,1,0:T(4,128)S(1)} %get-tuple-element.1461), channel_id=1, source_target_pairs={{0,4},{4,8},{8,12},{1,5},{5,9},{9,13},{2,6},{6,10},{10,14},{3,7},{... | collective-permute-start | bytes 393224 | tf_op jit(solution)/shard_map/while/body/eval_jaxpr/ppermute | solution.py:16
  80.9 18.9 %multiply_subtract_fusion.10 = (f32[2,4,8,512]{3,2,1,0:T(8,128)S(1)}, f32[2,4,8,512]{3,2,1,0:T(8,128)S(1)}, f32[2,4,8,512]{3,2,1,0:T(8,128)S(1)}) fusion(f32[4,8,512]{2,1,0:T(8,128)S(1)} %get-tuple-element.1360, f32[4,8,512]{2,1,0:T(8,128)S(1)} %get-tuple-element.1361, f32[4]{0:T(128)S(1)} %get-tuple-element.1362, f32[4]{0:T(128)S(1)} %get-tuple-element.1363, ...), kind=kLoop, calls=%fused_computation.173.clone.1 | loop fusion | flops 21757952 | bytes 2835456 | tf_op jit(solution)/shard_map/while/body/eval_jaxpr/sub | solution.py:45
  99.9 5.4 %collective-permute-start.2 = (f32[2,4,8,1024]{3,2,1,0:T(8,128)S(1)}, f32[2,4,8,1024]{3,2,1,0:T(8,128)S(1)}, u32[]{:S(2)}, u32[]{:S(2)}) collective-permute-start(f32[2,4,8,1024]{3,2,1,0:T(8,128)S(1)} %pad_maximum_fusion.17), channel_id=1, source_target_pairs={{0,1},{1,2},{2,3},{4,5},{5,6},{6,7},{8,9},{9,10},{10,11},{12,13},{... | collective-permute-start | bytes 786440 | tf_op jit(solution)/shard_map/while/body/eval_jaxpr/ppermute | solution.py:25
  107.9 4.7 %collective-permute-start.1 = (f32[2,4,4,1024]{3,2,1,0:T(4,128)S(1)}, f32[2,4,4,1024]{3,2,1,0:T(4,128)S(1)}, u32[]{:S(2)}, u32[]{:S(2)}) collective-permute-start(f32[2,4,4,1024]{3,2,1,0:T(4,128)S(1)} %get-tuple-element.1461), channel_id=1, source_target_pairs={{0,4},{4,8},{8,12},{1,5},{5,9},{9,13},{2,6},{6,10},{10,14},{3,7},{... | collective-permute-start | bytes 393224 | tf_op jit(solution)/shard_map/while/body/eval_jaxpr/ppermute | solution.py:16
  115.2 18.9 %multiply_subtract_fusion.10 = (f32[2,4,8,512]{3,2,1,0:T(8,128)S(1)}, f32[2,4,8,512]{3,2,1,0:T(8,128)S(1)}, f32[2,4,8,512]{3,2,1,0:T(8,128)S(1)}) fusion(f32[4,8,512]{2,1,0:T(8,128)S(1)} %get-tuple-element.1360, f32[4,8,512]{2,1,0:T(8,128)S(1)} %get-tuple-element.1361, f32[4]{0:T(128)S(1)} %get-tuple-element.1362, f32[4]{0:T(128)S(1)} %get-tuple-element.1363, ...), kind=kLoop, calls=%fused_computation.173.clone.1 | loop fusion | flops 21757952 | bytes 2835456 | tf_op jit(solution)/shard_map/while/body/eval_jaxpr/sub | solution.py:45
  134.3 6.9 %collective-permute-start.2 = (f32[2,4,8,1024]{3,2,1,0:T(8,128)S(1)}, f32[2,4,8,1024]{3,2,1,0:T(8,128)S(1)}, u32[]{:S(2)}, u32[]{:S(2)}) collective-permute-start(f32[2,4,8,1024]{3,2,1,0:T(8,128)S(1)} %pad_maximum_fusion.17), channel_id=1, source_target_pairs={{0,1},{1,2},{2,3},{4,5},{5,6},{6,7},{8,9},{9,10},{10,11},{12,13},{... | collective-permute-start | bytes 786440 | tf_op jit(solution)/shard_map/while/body/eval_jaxpr/ppermute | solution.py:25
  142.3 4.1 %collective-permute-start.6 = (f32[2,4,4,1024]{3,2,1,0:T(4,128)S(1)}, f32[2,4,4,1024]{3,2,1,0:T(4,128)S(1)}, u32[]{:S(2)}, u32[]{:S(2)}) collective-permute-start(f32[2,4,4,1024]{3,2,1,0:T(4,128)S(1)} %get-tuple-element.844), channel_id=1, source_target_pairs={{0,4},{4,8},{8,12},{1,5},{5,9},{9,13},{2,6},{6,10},{10,14},{3,7},{... | collective-permute-start | bytes 393224 | tf_op jit(solution)/shard_map/ppermute | solution.py:16
  153.5 19.0 %multiply_subtract_fusion.3 = (f32[2,4,8,512]{3,2,1,0:T(8,128)S(1)}, f32[2,4,8,512]{3,2,1,0:T(8,128)S(1)}, f32[2,4,8,512]{3,2,1,0:T(8,128)S(1)}) fusion(f32[4,8,512]{2,1,0:T(8,128)S(1)} %get-tuple-element.938, f32[4,8,512]{2,1,0:T(8,128)S(1)} %get-tuple-element.937, f32[4]{0:T(128)S(1)} %get-tuple-element.426, f32[4]{0:T(128)S(1)} %get-tuple-element.425, ...), kind=kLoop, calls=%fused_computation.1000 | loop fusion | flops 21757952 | bytes 2835456 | tf_op jit(solution)/shard_map/sub | solution.py:45
  172.5 72.3 %while.29 = (s32[]{:T(128)}, f32[1,4,8,1024]{3,2,1,0:T(8,128)S(1)}, f32[4,1,9,9]{0,3,2,1:T(8,128)S(1)}, f32[1,8,1024]{2,1,0:T(8,128)S(1)}, f32[1,4,8,1024]{3,2,1...) while((s32[]{:T(128)}, f32[1,4,8,1024]{3,2,1,0:T(8,128)S(1)}, ...), condition=%wide.region_4.5_spmd.clone.clone, body=%wide.region_3.4_spmd.clone.clone.sunk | while | flops 11239426 | bytes 7006565 | solution.py:128
  172.9 3.9 %collective-permute-start.3 = (f32[1,4,4,1024]{3,2,1,0:T(4,128)S(1)}, f32[1,4,4,1024]{3,2,1,0:T(4,128)S(1)}, u32[]{:S(2)}, u32[]{:S(2)}) collective-permute-start(f32[1,4,4,1024]{3,2,1,0:T(4,128)S(1)} %get-tuple-element.1541), channel_id=1, source_target_pairs={{0,4},{4,8},{8,12},{1,5},{5,9},{9,13},{2,6},{6,10},{10,14},{3,7},{... | collective-permute-start | bytes 196616 | tf_op jit(solution)/shard_map/while/body/eval_jaxpr/ppermute | solution.py:16
  178.7 4.3 %collective-permute-done.4 = f32[1,4,4,1024]{3,2,1,0:T(4,128)S(1)} collective-permute-done((f32[1,4,4,1024]{3,2,1,0:T(4,128)S(1)}, f32[1,4,4,1024]{3,2,1,0:T(4,128)S(1)}, u32[]{:S(2)}, u32[]{:S(2)}) %collective-permute-start.4) | collective-permute-done | bytes 65568 | tf_op jit(solution)/shard_map/while/body/eval_jaxpr/ppermute | solution.py:17
  183.2 3.7 %multiply_subtract_fusion.11 = f32[1,4,8,512]{3,2,1,0:T(8,128)S(1)} fusion(f32[1,4,8,512]{3,2,1,0:T(8,128)S(1)} %get-tuple-element.1539, f32[1,4,8,512]{3,2,1,0:T(8,128)S(1)} %get-tuple-element.1540, f32[1,4,12,1024]{3,2,1,0:T(8,128)S(1)} %get-tuple-element.1543, f32[1,4,12,1024]{3,2,1,0:T(8,128)S(1)} %get-tuple-element.1544, ...), kind=kLoop, calls=%fused_computation.510.clone.1 | loop fusion | flops 5292032 | bytes 1509920 | tf_op jit(solution)/shard_map/while/body/eval_jaxpr/sub | solution.py:72
  186.8 3.7 %multiply_add_fusion.21 = f32[1,4,8,512]{3,2,1,0:T(8,128)S(1)} fusion(f32[1,4,8,512]{3,2,1,0:T(8,128)S(1)} %get-tuple-element.1539, f32[1,4,8,512]{3,2,1,0:T(8,128)S(1)} %get-tuple-element.1540, f32[1,4,12,1024]{3,2,1,0:T(8,128)S(1)} %get-tuple-element.1543, f32[1,4,12,1024]{3,2,1,0:T(8,128)S(1)} %get-tuple-element.1544, ...), kind=kLoop, calls=%fused_computation.508.clone.1 | loop fusion | flops 5292032 | bytes 1509920 | tf_op jit(solution)/shard_map/while/body/eval_jaxpr/add | solution.py:73
  191.8 4.9 %collective-permute-done.5 = f32[1,4,8,1024]{3,2,1,0:T(8,128)S(1)} collective-permute-done((f32[1,4,8,1024]{3,2,1,0:T(8,128)S(1)}, f32[1,4,8,1024]{3,2,1,0:T(8,128)S(1)}, u32[]{:S(2)}, u32[]{:S(2)}) %collective-permute-start.5) | collective-permute-done | bytes 131104 | tf_op jit(solution)/shard_map/while/body/eval_jaxpr/ppermute | solution.py:25
  197.1 3.6 %collective-permute-start.3 = (f32[1,4,4,1024]{3,2,1,0:T(4,128)S(1)}, f32[1,4,4,1024]{3,2,1,0:T(4,128)S(1)}, u32[]{:S(2)}, u32[]{:S(2)}) collective-permute-start(f32[1,4,4,1024]{3,2,1,0:T(4,128)S(1)} %get-tuple-element.1541), channel_id=1, source_target_pairs={{0,4},{4,8},{8,12},{1,5},{5,9},{9,13},{2,6},{6,10},{10,14},{3,7},{... | collective-permute-start | bytes 196616 | tf_op jit(solution)/shard_map/while/body/eval_jaxpr/ppermute | solution.py:16
  202.6 4.3 %collective-permute-done.4 = f32[1,4,4,1024]{3,2,1,0:T(4,128)S(1)} collective-permute-done((f32[1,4,4,1024]{3,2,1,0:T(4,128)S(1)}, f32[1,4,4,1024]{3,2,1,0:T(4,128)S(1)}, u32[]{:S(2)}, u32[]{:S(2)}) %collective-permute-start.4) | collective-permute-done | bytes 65568 | tf_op jit(solution)/shard_map/while/body/eval_jaxpr/ppermute | solution.py:17
  207.0 3.7 %multiply_subtract_fusion.11 = f32[1,4,8,512]{3,2,1,0:T(8,128)S(1)} fusion(f32[1,4,8,512]{3,2,1,0:T(8,128)S(1)} %get-tuple-element.1539, f32[1,4,8,512]{3,2,1,0:T(8,128)S(1)} %get-tuple-element.1540, f32[1,4,12,1024]{3,2,1,0:T(8,128)S(1)} %get-tuple-element.1543, f32[1,4,12,1024]{3,2,1,0:T(8,128)S(1)} %get-tuple-element.1544, ...), kind=kLoop, calls=%fused_computation.510.clone.1 | loop fusion | flops 5292032 | bytes 1509920 | tf_op jit(solution)/shard_map/while/body/eval_jaxpr/sub | solution.py:72
  210.7 3.7 %multiply_add_fusion.21 = f32[1,4,8,512]{3,2,1,0:T(8,128)S(1)} fusion(f32[1,4,8,512]{3,2,1,0:T(8,128)S(1)} %get-tuple-element.1539, f32[1,4,8,512]{3,2,1,0:T(8,128)S(1)} %get-tuple-element.1540, f32[1,4,12,1024]{3,2,1,0:T(8,128)S(1)} %get-tuple-element.1543, f32[1,4,12,1024]{3,2,1,0:T(8,128)S(1)} %get-tuple-element.1544, ...), kind=kLoop, calls=%fused_computation.508.clone.1 | loop fusion | flops 5292032 | bytes 1509920 | tf_op jit(solution)/shard_map/while/body/eval_jaxpr/add | solution.py:73
  215.7 6.9 %collective-permute-done.5 = f32[1,4,8,1024]{3,2,1,0:T(8,128)S(1)} collective-permute-done((f32[1,4,8,1024]{3,2,1,0:T(8,128)S(1)}, f32[1,4,8,1024]{3,2,1,0:T(8,128)S(1)}, u32[]{:S(2)}, u32[]{:S(2)}) %collective-permute-start.5) | collective-permute-done | bytes 131104 | tf_op jit(solution)/shard_map/while/body/eval_jaxpr/ppermute | solution.py:25
  228.2 4.3 %collective-permute-done.4 = f32[1,4,4,1024]{3,2,1,0:T(4,128)S(1)} collective-permute-done((f32[1,4,4,1024]{3,2,1,0:T(4,128)S(1)}, f32[1,4,4,1024]{3,2,1,0:T(4,128)S(1)}, u32[]{:S(2)}, u32[]{:S(2)}) %collective-permute-start.4) | collective-permute-done | bytes 65568 | tf_op jit(solution)/shard_map/while/body/eval_jaxpr/ppermute | solution.py:17
  232.6 3.7 %multiply_subtract_fusion.11 = f32[1,4,8,512]{3,2,1,0:T(8,128)S(1)} fusion(f32[1,4,8,512]{3,2,1,0:T(8,128)S(1)} %get-tuple-element.1539, f32[1,4,8,512]{3,2,1,0:T(8,128)S(1)} %get-tuple-element.1540, f32[1,4,12,1024]{3,2,1,0:T(8,128)S(1)} %get-tuple-element.1543, f32[1,4,12,1024]{3,2,1,0:T(8,128)S(1)} %get-tuple-element.1544, ...), kind=kLoop, calls=%fused_computation.510.clone.1 | loop fusion | flops 5292032 | bytes 1509920 | tf_op jit(solution)/shard_map/while/body/eval_jaxpr/sub | solution.py:72
  236.3 3.7 %multiply_add_fusion.21 = f32[1,4,8,512]{3,2,1,0:T(8,128)S(1)} fusion(f32[1,4,8,512]{3,2,1,0:T(8,128)S(1)} %get-tuple-element.1539, f32[1,4,8,512]{3,2,1,0:T(8,128)S(1)} %get-tuple-element.1540, f32[1,4,12,1024]{3,2,1,0:T(8,128)S(1)} %get-tuple-element.1543, f32[1,4,12,1024]{3,2,1,0:T(8,128)S(1)} %get-tuple-element.1544, ...), kind=kLoop, calls=%fused_computation.508.clone.1 | loop fusion | flops 5292032 | bytes 1509920 | tf_op jit(solution)/shard_map/while/body/eval_jaxpr/add | solution.py:73
  241.2 3.6 %collective-permute-done.5 = f32[1,4,8,1024]{3,2,1,0:T(8,128)S(1)} collective-permute-done((f32[1,4,8,1024]{3,2,1,0:T(8,128)S(1)}, f32[1,4,8,1024]{3,2,1,0:T(8,128)S(1)}, u32[]{:S(2)}, u32[]{:S(2)}) %collective-permute-start.5) | collective-permute-done | bytes 131104 | tf_op jit(solution)/shard_map/while/body/eval_jaxpr/ppermute | solution.py:25
  249.3 4.5 %collective-permute-done.9 = f32[1,4,4,1024]{3,2,1,0:T(4,128)S(1)} collective-permute-done((f32[1,4,4,1024]{3,2,1,0:T(4,128)S(1)}, f32[1,4,4,1024]{3,2,1,0:T(4,128)S(1)}, u32[]{:S(2)}, u32[]{:S(2)}) %collective-permute-start.9) | collective-permute-done | bytes 65568 | tf_op jit(solution)/shard_map/ppermute | solution.py:17
  253.9 3.7 %multiply_subtract_fusion.5 = f32[1,4,8,512]{3,2,1,0:T(8,128)S(1)} fusion(f32[1,4,8,512]{3,2,1,0:T(8,128)S(1)} %get-tuple-element.847, f32[1,4,8,512]{3,2,1,0:T(8,128)S(1)} %get-tuple-element.846, f32[1,4,12,1024]{3,2,1,0:T(8,128)S(1)} %get-tuple-element.851, f32[1,4,12,1024]{3,2,1,0:T(8,128)S(1)} %get-tuple-element.850, ...), kind=kLoop, calls=%fused_computation.1023 | loop fusion | flops 5292032 | bytes 1509920 | tf_op jit(solution)/shard_map/sub | solution.py:72
  257.5 3.7 %multiply_add_fusion.13 = f32[1,4,8,512]{3,2,1,0:T(8,128)S(1)} fusion(f32[1,4,8,512]{3,2,1,0:T(8,128)S(1)} %get-tuple-element.847, f32[1,4,8,512]{3,2,1,0:T(8,128)S(1)} %get-tuple-element.846, f32[1,4,12,1024]{3,2,1,0:T(8,128)S(1)} %get-tuple-element.851, f32[1,4,12,1024]{3,2,1,0:T(8,128)S(1)} %get-tuple-element.850, ...), kind=kLoop, calls=%fused_computation.1021 | loop fusion | flops 5292032 | bytes 1509920 | tf_op jit(solution)/shard_map/add | solution.py:73
  262.5 30.9 %all-reduce.11.cloned.1.call-done = f32[4,8,1024]{2,1,0:T(8,128)} async-done(((f32[4,8,1024]{2,1,0:T(8,128)}), f32[4,8,1024]{2,1,0:T(8,128)}) %all-reduce.11.cloned.1.call-update) | async-done | bytes 131088 | tf_op jit(solution)/shard_map/psum | solution.py:30
  (203 shorter events, 50.5 us)
Async XLA Ops:
  7.2 286.3 %all-reduce.11.cloned.1.call-start = ((), (), s32[]{:S(2)}) async-start(), calls=%async_computation | async-start | bytes 262144 | tf_op jit(solution)/shard_map/psum | solution.py:30
  7.2 0.7 copy-start.7
  9.1 0.7 copy-start.5
  9.1 0.7 copy-start.6
  38.7 0.9 copy-start.1
  39.7 0.7 copy-start.4
  39.7 1.4 copy-start
  41.1 0.7 copy-start.2
  41.8 6.9 %collective-permute-start = (f32[2,4,4,1024]{3,2,1,0:T(4,128)S(1)}, f32[2,4,4,1024]{3,2,1,0:T(4,128)S(1)}, u32[]{:S(2)}, u32[]{:S(2)}) collective-permute-start(f32[2,4,4,1024]{3,2,1,0:T(4,128)S(1)} %get-tuple-element.1370), channel_id=1, source_target_pairs={{4,0},{8,4},{12,8},{5,1},{9,5},{13,9},{6,2},{10,6},{14,10},{7,3},{... | collective-permute-start | bytes 393224 | tf_op jit(solution)/shard_map/while/body/eval_jaxpr/ppermute | solution.py:17
  43.1 7.1 %collective-permute-start.1 = (f32[2,4,4,1024]{3,2,1,0:T(4,128)S(1)}, f32[2,4,4,1024]{3,2,1,0:T(4,128)S(1)}, u32[]{:S(2)}, u32[]{:S(2)}) collective-permute-start(f32[2,4,4,1024]{3,2,1,0:T(4,128)S(1)} %get-tuple-element.1461), channel_id=1, source_target_pairs={{0,4},{4,8},{8,12},{1,5},{5,9},{9,13},{2,6},{6,10},{10,14},{3,7},{... | collective-permute-start | bytes 393224 | tf_op jit(solution)/shard_map/while/body/eval_jaxpr/ppermute | solution.py:16
  69.4 2.4 collective-permute-start.2
  71.9 7.3 %collective-permute-start = (f32[2,4,4,1024]{3,2,1,0:T(4,128)S(1)}, f32[2,4,4,1024]{3,2,1,0:T(4,128)S(1)}, u32[]{:S(2)}, u32[]{:S(2)}) collective-permute-start(f32[2,4,4,1024]{3,2,1,0:T(4,128)S(1)} %get-tuple-element.1370), channel_id=1, source_target_pairs={{4,0},{8,4},{12,8},{5,1},{9,5},{13,9},{6,2},{10,6},{14,10},{7,3},{... | collective-permute-start | bytes 393224 | tf_op jit(solution)/shard_map/while/body/eval_jaxpr/ppermute | solution.py:17
  73.2 7.5 %collective-permute-start.1 = (f32[2,4,4,1024]{3,2,1,0:T(4,128)S(1)}, f32[2,4,4,1024]{3,2,1,0:T(4,128)S(1)}, u32[]{:S(2)}, u32[]{:S(2)}) collective-permute-start(f32[2,4,4,1024]{3,2,1,0:T(4,128)S(1)} %get-tuple-element.1461), channel_id=1, source_target_pairs={{0,4},{4,8},{8,12},{1,5},{5,9},{9,13},{2,6},{6,10},{10,14},{3,7},{... | collective-permute-start | bytes 393224 | tf_op jit(solution)/shard_map/while/body/eval_jaxpr/ppermute | solution.py:16
  99.9 6.6 %collective-permute-start.2 = (f32[2,4,8,1024]{3,2,1,0:T(8,128)S(1)}, f32[2,4,8,1024]{3,2,1,0:T(8,128)S(1)}, u32[]{:S(2)}, u32[]{:S(2)}) collective-permute-start(f32[2,4,8,1024]{3,2,1,0:T(8,128)S(1)} %pad_maximum_fusion.17), channel_id=1, source_target_pairs={{0,1},{1,2},{2,3},{4,5},{5,6},{6,7},{8,9},{9,10},{10,11},{12,13},{... | collective-permute-start | bytes 786440 | tf_op jit(solution)/shard_map/while/body/eval_jaxpr/ppermute | solution.py:25
  106.6 7.0 %collective-permute-start = (f32[2,4,4,1024]{3,2,1,0:T(4,128)S(1)}, f32[2,4,4,1024]{3,2,1,0:T(4,128)S(1)}, u32[]{:S(2)}, u32[]{:S(2)}) collective-permute-start(f32[2,4,4,1024]{3,2,1,0:T(4,128)S(1)} %get-tuple-element.1370), channel_id=1, source_target_pairs={{4,0},{8,4},{12,8},{5,1},{9,5},{13,9},{6,2},{10,6},{14,10},{7,3},{... | collective-permute-start | bytes 393224 | tf_op jit(solution)/shard_map/while/body/eval_jaxpr/ppermute | solution.py:17
  107.9 7.2 %collective-permute-start.1 = (f32[2,4,4,1024]{3,2,1,0:T(4,128)S(1)}, f32[2,4,4,1024]{3,2,1,0:T(4,128)S(1)}, u32[]{:S(2)}, u32[]{:S(2)}) collective-permute-start(f32[2,4,4,1024]{3,2,1,0:T(4,128)S(1)} %get-tuple-element.1461), channel_id=1, source_target_pairs={{0,4},{4,8},{8,12},{1,5},{5,9},{9,13},{2,6},{6,10},{10,14},{3,7},{... | collective-permute-start | bytes 393224 | tf_op jit(solution)/shard_map/while/body/eval_jaxpr/ppermute | solution.py:16
  134.3 8.0 %collective-permute-start.2 = (f32[2,4,8,1024]{3,2,1,0:T(8,128)S(1)}, f32[2,4,8,1024]{3,2,1,0:T(8,128)S(1)}, u32[]{:S(2)}, u32[]{:S(2)}) collective-permute-start(f32[2,4,8,1024]{3,2,1,0:T(8,128)S(1)} %pad_maximum_fusion.17), channel_id=1, source_target_pairs={{0,1},{1,2},{2,3},{4,5},{5,6},{6,7},{8,9},{9,10},{10,11},{12,13},{... | collective-permute-start | bytes 786440 | tf_op jit(solution)/shard_map/while/body/eval_jaxpr/ppermute | solution.py:25
  142.3 9.4 %collective-permute-start.6 = (f32[2,4,4,1024]{3,2,1,0:T(4,128)S(1)}, f32[2,4,4,1024]{3,2,1,0:T(4,128)S(1)}, u32[]{:S(2)}, u32[]{:S(2)}) collective-permute-start(f32[2,4,4,1024]{3,2,1,0:T(4,128)S(1)} %get-tuple-element.844), channel_id=1, source_target_pairs={{0,4},{4,8},{8,12},{1,5},{5,9},{9,13},{2,6},{6,10},{10,14},{3,7},{... | collective-permute-start | bytes 393224 | tf_op jit(solution)/shard_map/ppermute | solution.py:16
  146.4 6.9 %collective-permute-start.7 = (f32[2,4,4,1024]{3,2,1,0:T(4,128)S(1)}, f32[2,4,4,1024]{3,2,1,0:T(4,128)S(1)}, u32[]{:S(2)}, u32[]{:S(2)}) collective-permute-start(f32[2,4,4,1024]{3,2,1,0:T(4,128)S(1)} %get-tuple-element.845), channel_id=1, source_target_pairs={{4,0},{8,4},{12,8},{5,1},{9,5},{13,9},{6,2},{10,6},{14,10},{7,3},{... | collective-permute-start | bytes 393224 | tf_op jit(solution)/shard_map/ppermute | solution.py:17
  150.7 0.7 copy-start.3
  172.9 5.8 %collective-permute-start.3 = (f32[1,4,4,1024]{3,2,1,0:T(4,128)S(1)}, f32[1,4,4,1024]{3,2,1,0:T(4,128)S(1)}, u32[]{:S(2)}, u32[]{:S(2)}) collective-permute-start(f32[1,4,4,1024]{3,2,1,0:T(4,128)S(1)} %get-tuple-element.1541), channel_id=1, source_target_pairs={{0,4},{4,8},{8,12},{1,5},{5,9},{9,13},{2,6},{6,10},{10,14},{3,7},{... | collective-permute-start | bytes 196616 | tf_op jit(solution)/shard_map/while/body/eval_jaxpr/ppermute | solution.py:16
  176.9 6.2 %collective-permute-start.4 = (f32[1,4,4,1024]{3,2,1,0:T(4,128)S(1)}, f32[1,4,4,1024]{3,2,1,0:T(4,128)S(1)}, u32[]{:S(2)}, u32[]{:S(2)}) collective-permute-start(f32[1,4,4,1024]{3,2,1,0:T(4,128)S(1)} %get-tuple-element.1542), channel_id=1, source_target_pairs={{4,0},{8,4},{12,8},{5,1},{9,5},{13,9},{6,2},{10,6},{14,10},{7,3},{... | collective-permute-start | bytes 196616 | tf_op jit(solution)/shard_map/while/body/eval_jaxpr/ppermute | solution.py:17
  190.5 6.2 %collective-permute-start.5 = (f32[1,4,8,1024]{3,2,1,0:T(8,128)S(1)}, f32[1,4,8,1024]{3,2,1,0:T(8,128)S(1)}, u32[]{:S(2)}, u32[]{:S(2)}) collective-permute-start(f32[1,4,8,1024]{3,2,1,0:T(8,128)S(1)} %pad_maximum_fusion.19), channel_id=1, source_target_pairs={{1,0},{2,1},{3,2},{5,4},{6,5},{7,6},{9,8},{10,9},{11,10},{13,12},{... | collective-permute-start | bytes 393224 | tf_op jit(solution)/shard_map/while/body/eval_jaxpr/ppermute | solution.py:25
  197.1 5.5 %collective-permute-start.3 = (f32[1,4,4,1024]{3,2,1,0:T(4,128)S(1)}, f32[1,4,4,1024]{3,2,1,0:T(4,128)S(1)}, u32[]{:S(2)}, u32[]{:S(2)}) collective-permute-start(f32[1,4,4,1024]{3,2,1,0:T(4,128)S(1)} %get-tuple-element.1541), channel_id=1, source_target_pairs={{0,4},{4,8},{8,12},{1,5},{5,9},{9,13},{2,6},{6,10},{10,14},{3,7},{... | collective-permute-start | bytes 196616 | tf_op jit(solution)/shard_map/while/body/eval_jaxpr/ppermute | solution.py:16
  200.7 6.2 %collective-permute-start.4 = (f32[1,4,4,1024]{3,2,1,0:T(4,128)S(1)}, f32[1,4,4,1024]{3,2,1,0:T(4,128)S(1)}, u32[]{:S(2)}, u32[]{:S(2)}) collective-permute-start(f32[1,4,4,1024]{3,2,1,0:T(4,128)S(1)} %get-tuple-element.1542), channel_id=1, source_target_pairs={{4,0},{8,4},{12,8},{5,1},{9,5},{13,9},{6,2},{10,6},{14,10},{7,3},{... | collective-permute-start | bytes 196616 | tf_op jit(solution)/shard_map/while/body/eval_jaxpr/ppermute | solution.py:17
  214.4 8.2 %collective-permute-start.5 = (f32[1,4,8,1024]{3,2,1,0:T(8,128)S(1)}, f32[1,4,8,1024]{3,2,1,0:T(8,128)S(1)}, u32[]{:S(2)}, u32[]{:S(2)}) collective-permute-start(f32[1,4,8,1024]{3,2,1,0:T(8,128)S(1)} %pad_maximum_fusion.19), channel_id=1, source_target_pairs={{1,0},{2,1},{3,2},{5,4},{6,5},{7,6},{9,8},{10,9},{11,10},{13,12},{... | collective-permute-start | bytes 393224 | tf_op jit(solution)/shard_map/while/body/eval_jaxpr/ppermute | solution.py:25
  223.0 5.2 %collective-permute-start.3 = (f32[1,4,4,1024]{3,2,1,0:T(4,128)S(1)}, f32[1,4,4,1024]{3,2,1,0:T(4,128)S(1)}, u32[]{:S(2)}, u32[]{:S(2)}) collective-permute-start(f32[1,4,4,1024]{3,2,1,0:T(4,128)S(1)} %get-tuple-element.1541), channel_id=1, source_target_pairs={{0,4},{4,8},{8,12},{1,5},{5,9},{9,13},{2,6},{6,10},{10,14},{3,7},{... | collective-permute-start | bytes 196616 | tf_op jit(solution)/shard_map/while/body/eval_jaxpr/ppermute | solution.py:16
  226.3 6.2 %collective-permute-start.4 = (f32[1,4,4,1024]{3,2,1,0:T(4,128)S(1)}, f32[1,4,4,1024]{3,2,1,0:T(4,128)S(1)}, u32[]{:S(2)}, u32[]{:S(2)}) collective-permute-start(f32[1,4,4,1024]{3,2,1,0:T(4,128)S(1)} %get-tuple-element.1542), channel_id=1, source_target_pairs={{4,0},{8,4},{12,8},{5,1},{9,5},{13,9},{6,2},{10,6},{14,10},{7,3},{... | collective-permute-start | bytes 196616 | tf_op jit(solution)/shard_map/while/body/eval_jaxpr/ppermute | solution.py:17
  239.9 4.9 %collective-permute-start.5 = (f32[1,4,8,1024]{3,2,1,0:T(8,128)S(1)}, f32[1,4,8,1024]{3,2,1,0:T(8,128)S(1)}, u32[]{:S(2)}, u32[]{:S(2)}) collective-permute-start(f32[1,4,8,1024]{3,2,1,0:T(8,128)S(1)} %pad_maximum_fusion.19), channel_id=1, source_target_pairs={{1,0},{2,1},{3,2},{5,4},{6,5},{7,6},{9,8},{10,9},{11,10},{13,12},{... | collective-permute-start | bytes 393224 | tf_op jit(solution)/shard_map/while/body/eval_jaxpr/ppermute | solution.py:25
  245.2 4.1 %collective-permute-start.8 = (f32[1,4,4,1024]{3,2,1,0:T(4,128)S(1)}, f32[1,4,4,1024]{3,2,1,0:T(4,128)S(1)}, u32[]{:S(2)}, u32[]{:S(2)}) collective-permute-start(f32[1,4,4,1024]{3,2,1,0:T(4,128)S(1)} %get-tuple-element.852), channel_id=1, source_target_pairs={{0,4},{4,8},{8,12},{1,5},{5,9},{9,13},{2,6},{6,10},{10,14},{3,7},{... | collective-permute-start | bytes 196616 | tf_op jit(solution)/shard_map/ppermute | solution.py:16
  247.6 6.2 %collective-permute-start.9 = (f32[1,4,4,1024]{3,2,1,0:T(4,128)S(1)}, f32[1,4,4,1024]{3,2,1,0:T(4,128)S(1)}, u32[]{:S(2)}, u32[]{:S(2)}) collective-permute-start(f32[1,4,4,1024]{3,2,1,0:T(4,128)S(1)} %get-tuple-element.853), channel_id=1, source_target_pairs={{4,0},{8,4},{12,8},{5,1},{9,5},{13,9},{6,2},{10,6},{14,10},{7,3},{... | collective-permute-start | bytes 196616 | tf_op jit(solution)/shard_map/ppermute | solution.py:17
Sparse Core Ops, SparseCore 0:
  262.0 31.4 all-reduce.10
where the time goes:
time: 303 us; the launch traced here: 302 us
  other arithmetic  111 us (37%)
  waiting for transfers between devices  76.1 us (25%)
  starting transfers between devices  59.4 us (20%)
  blocking collectives  28.5 us (9%)
  between operations  15.1 us (5%)
  local copies, waits for them, and re-layouts  10.2 us (3%)
    sub x8, other arithmetic, rotate(): real_part * cosine - imag_part * sine_part  77.1 us
    ppermute x8, starting transfers between devices, padded_2(): before = lax.ppermute(last, axis, up)  31.5 us
    psum x1, waiting for transfers between devices, broadcast(): return lax.psum(block, axis)  30.9 us
    ppermute x8, waiting for transfers between devices, padded_2(): after = lax.ppermute(leading, axis, down)  20.3 us
    ppermute x6, waiting for transfers between devices, from_behind(): lax.ppermute(value, axis, [(source, source + steps) for source in range(l...  18.7 us
    ppermute x6, starting transfers between devices, from_behind(): lax.ppermute(value, axis, [(source, source + steps) for source in range(l...  17.5 us
    all_gather x1, blocking collectives, local(): piece_traces = lax.all_gather(traces, 'lat', axis=0, tiled=True)  15 us
    add x4, other arithmetic, convolve(): out_imag = out_imag + tap_imag * real_piece + tap_real * imag_piece  14.6 us
  transfers between devices with their start and end apart: 23, of which 22 were waited for; matrix products, arithmetic and copies ran while one was open for 2% of the time, Pallas kernels for 0%

commit v1 on v0

--- a/solution.py
+++ b/solution.py
@@ -4,6 +4,10 @@
 from jax.sharding import PartitionSpec as P
 
 precision_high = lax.Precision.HIGHEST
+
+
+def perform_gates_here(sample, mesh_dim):
+    return jnp.sum(lax.all_gather(sample, axis_name=mesh_dim), 0)
 
 
 def padded_2(array, sides, width):
@@ -27,7 +31,7 @@
 
 def broadcast(block, axis, holder):
     block = jnp.where(lax.axis_index(axis) == holder, block, jnp.zeros_like(block))
-    return lax.psum(block, axis)
+    return perform_gates_here(block, axis)
 
 
 def make_taps(stencil):

time: 303 us -> 265 us (0.87)
  waiting for transfers between devices: 76.1 us -> 44.3 us
  between operations: 15.1 us -> 1.71 us
  blocking collectives: 28.5 us -> 37.6 us
    psum x1 -> x0, waiting for transfers between devices: 30.9 us -> none  [broadcast(): return lax.psum(block, axis)]
    all_gather x0 -> x1, blocking collectives: none -> 9.06 us  [perform_gates_here(): return jnp.sum(lax.all_gather(sample, axis_name=mesh_dim), 0)]
  transfers between devices with their start and end apart: 23 -> 22, of which waited for: 22 -> 20; matrix products, arithmetic and copies ran while one was open for 2% -> 2% of each run, Pallas kernels for 0% -> 0%
where the time goes in v1:
time: 265 us; the launch traced here: 264 us
  other arithmetic  110 us (42%)
  starting transfers between devices  59.4 us (22%)
  waiting for transfers between devices  44.3 us (17%)
  blocking collectives  37.6 us (14%)
  local copies, waits for them, and re-layouts  10.2 us (4%)
    sub x8, other arithmetic, rotate(): real_part * cosine - imag_part * sine_part  77.1 us
    ppermute x8, starting transfers between devices, padded_2(): before = lax.ppermute(last, axis, up)  31.4 us
    ppermute x8, waiting for transfers between devices, padded_2(): after = lax.ppermute(leading, axis, down)  19.8 us
    ppermute x6, waiting for transfers between devices, from_behind(): lax.ppermute(value, axis, [(source, source + steps) for source in range(l...  18.7 us
    ppermute x6, starting transfers between devices, from_behind(): lax.ppermute(value, axis, [(source, source + steps) for source in range(l...  17.5 us
    all_gather x1, blocking collectives, local(): piece_traces = lax.all_gather(traces, 'lat', axis=0, tiled=True)  15 us
    add x4, other arithmetic, convolve(): out_imag = out_imag + tap_imag * real_piece + tap_real * imag_piece  14.6 us
    sub x4, other arithmetic, convolve(): out_real = out_real + tap_real * real_piece - tap_imag * imag_piece  14.6 us
  transfers between devices with their start and end apart: 22, of which 20 were waited for; matrix products, arithmetic and copies ran while one was open for 2% of the time, Pallas kernels for 0%

profile of v1, /device:TPU:0, one launch (start us, length us, event | category | flops | bytes accessed | tf_op | source)
XLA Modules:
  0.0 264.2 jit_solution(6957278127998083286)
XLA Ops:
  3.3 13.5 %all-reduce.8 = f32[32]{0:T(128)S(1)} all-reduce(f32[32]{0:T(128)S(1)} %fusion.47), channel_id=1, replica_groups=mesh['shots'=2,'lat'=4,'depth'=4] {'lat'}, use_global_device_ids=true, to_apply=%add.8 | all-reduce | flops 32 | bytes 256
  16.8 15.0 %all_gather.11 = f32[32,4096]{1,0:T(8,128)S(1)} all-gather(f32[8,4096]{1,0:T(8,128)} %param.13), channel_id=1, replica_groups=mesh['shots'=2,'lat'=4,'depth'=4] {'lat'}, dimensions={0}, use_global_device_ids=true | all-gather | bytes 655360 | tf_op jit(solution)/shard_map/all_gather | solution.py:104
  35.2 100.5 %while.28 = (s32[]{:T(128)}, f32[2,4,8,1024]{3,2,1,0:T(8,128)S(1)}, f32[4,2,9,9]{0,3,2,1:T(8,128)S(1)}, f32[2,4,8,1024]{3,2,1,0:T(8,128)S(1)}, f32[8,512]{1,0:T(8,128)S(1)}, /*index=5*/f32[4]{0:T(128)S(1)}, s32[]{:T(128)}) while((s32[]{:T(128)}, f32[2,4,8,1024]{3,2,1,0:T(8,128)S(1)}, f32[4,2,9,9]{0,3,2,1:T(8,128)S(1)}, ...), condition=%wide.region_1.2_spmd.clone.clone, body=%wide.region_0.1_spmd.clone.clone.sunk | while | flops 22265856 | bytes 10328341 | solution.py:123
  36.5 4.6 %collective-permute-start.1 = (f32[2,4,4,1024]{3,2,1,0:T(4,128)S(1)}, f32[2,4,4,1024]{3,2,1,0:T(4,128)S(1)}, u32[]{:S(2)}, u32[]{:S(2)}) collective-permute-start(f32[2,4,4,1024]{3,2,1,0:T(4,128)S(1)} %get-tuple-element.1445), channel_id=1, source_target_pairs={{0,4},{4,8},{8,12},{1,5},{5,9},{9,13},{2,6},{6,10},{10,14},{3,7},{... | collective-permute-start | bytes 393224 | tf_op jit(solution)/shard_map/while/body/eval_jaxpr/ppermute | solution.py:20
  43.8 18.9 %multiply_subtract_fusion.10 = (f32[2,4,8,512]{3,2,1,0:T(8,128)S(1)}, f32[2,4,8,512]{3,2,1,0:T(8,128)S(1)}, f32[2,4,8,512]{3,2,1,0:T(8,128)S(1)}) fusion(f32[4,8,512]{2,1,0:T(8,128)S(1)} %get-tuple-element.1344, f32[4,8,512]{2,1,0:T(8,128)S(1)} %get-tuple-element.1345, f32[4]{0:T(128)S(1)} %get-tuple-element.1346, f32[4]{0:T(128)S(1)} %get-tuple-element.1347, ...), kind=kLoop, calls=%fused_computation.173.clone.1 | loop fusion | flops 21757952 | bytes 2835456 | tf_op jit(solution)/shard_map/while/body/eval_jaxpr/sub | solution.py:49
  66.6 5.0 %collective-permute-start.1 = (f32[2,4,4,1024]{3,2,1,0:T(4,128)S(1)}, f32[2,4,4,1024]{3,2,1,0:T(4,128)S(1)}, u32[]{:S(2)}, u32[]{:S(2)}) collective-permute-start(f32[2,4,4,1024]{3,2,1,0:T(4,128)S(1)} %get-tuple-element.1445), channel_id=1, source_target_pairs={{0,4},{4,8},{8,12},{1,5},{5,9},{9,13},{2,6},{6,10},{10,14},{3,7},{... | collective-permute-start | bytes 393224 | tf_op jit(solution)/shard_map/while/body/eval_jaxpr/ppermute | solution.py:20
  74.3 18.9 %multiply_subtract_fusion.10 = (f32[2,4,8,512]{3,2,1,0:T(8,128)S(1)}, f32[2,4,8,512]{3,2,1,0:T(8,128)S(1)}, f32[2,4,8,512]{3,2,1,0:T(8,128)S(1)}) fusion(f32[4,8,512]{2,1,0:T(8,128)S(1)} %get-tuple-element.1344, f32[4,8,512]{2,1,0:T(8,128)S(1)} %get-tuple-element.1345, f32[4]{0:T(128)S(1)} %get-tuple-element.1346, f32[4]{0:T(128)S(1)} %get-tuple-element.1347, ...), kind=kLoop, calls=%fused_computation.173.clone.1 | loop fusion | flops 21757952 | bytes 2835456 | tf_op jit(solution)/shard_map/while/body/eval_jaxpr/sub | solution.py:49
  93.3 5.4 %collective-permute-start.2 = (f32[2,4,8,1024]{3,2,1,0:T(8,128)S(1)}, f32[2,4,8,1024]{3,2,1,0:T(8,128)S(1)}, u32[]{:S(2)}, u32[]{:S(2)}) collective-permute-start(f32[2,4,8,1024]{3,2,1,0:T(8,128)S(1)} %pad_maximum_fusion.17), channel_id=1, source_target_pairs={{0,1},{1,2},{2,3},{4,5},{5,6},{6,7},{8,9},{9,10},{10,11},{12,13},{... | collective-permute-start | bytes 786440 | tf_op jit(solution)/shard_map/while/body/eval_jaxpr/ppermute | solution.py:29
  101.3 4.7 %collective-permute-start.1 = (f32[2,4,4,1024]{3,2,1,0:T(4,128)S(1)}, f32[2,4,4,1024]{3,2,1,0:T(4,128)S(1)}, u32[]{:S(2)}, u32[]{:S(2)}) collective-permute-start(f32[2,4,4,1024]{3,2,1,0:T(4,128)S(1)} %get-tuple-element.1445), channel_id=1, source_target_pairs={{0,4},{4,8},{8,12},{1,5},{5,9},{9,13},{2,6},{6,10},{10,14},{3,7},{... | collective-permute-start | bytes 393224 | tf_op jit(solution)/shard_map/while/body/eval_jaxpr/ppermute | solution.py:20
  108.7 18.9 %multiply_subtract_fusion.10 = (f32[2,4,8,512]{3,2,1,0:T(8,128)S(1)}, f32[2,4,8,512]{3,2,1,0:T(8,128)S(1)}, f32[2,4,8,512]{3,2,1,0:T(8,128)S(1)}) fusion(f32[4,8,512]{2,1,0:T(8,128)S(1)} %get-tuple-element.1344, f32[4,8,512]{2,1,0:T(8,128)S(1)} %get-tuple-element.1345, f32[4]{0:T(128)S(1)} %get-tuple-element.1346, f32[4]{0:T(128)S(1)} %get-tuple-element.1347, ...), kind=kLoop, calls=%fused_computation.173.clone.1 | loop fusion | flops 21757952 | bytes 2835456 | tf_op jit(solution)/shard_map/while/body/eval_jaxpr/sub | solution.py:49
  127.7 6.9 %collective-permute-start.2 = (f32[2,4,8,1024]{3,2,1,0:T(8,128)S(1)}, f32[2,4,8,1024]{3,2,1,0:T(8,128)S(1)}, u32[]{:S(2)}, u32[]{:S(2)}) collective-permute-start(f32[2,4,8,1024]{3,2,1,0:T(8,128)S(1)} %pad_maximum_fusion.17), channel_id=1, source_target_pairs={{0,1},{1,2},{2,3},{4,5},{5,6},{6,7},{8,9},{9,10},{10,11},{12,13},{... | collective-permute-start | bytes 786440 | tf_op jit(solution)/shard_map/while/body/eval_jaxpr/ppermute | solution.py:29
  135.8 4.1 %collective-permute-start.6 = (f32[2,4,4,1024]{3,2,1,0:T(4,128)S(1)}, f32[2,4,4,1024]{3,2,1,0:T(4,128)S(1)}, u32[]{:S(2)}, u32[]{:S(2)}) collective-permute-start(f32[2,4,4,1024]{3,2,1,0:T(4,128)S(1)} %get-tuple-element.828), channel_id=1, source_target_pairs={{0,4},{4,8},{8,12},{1,5},{5,9},{9,13},{2,6},{6,10},{10,14},{3,7},{... | collective-permute-start | bytes 393224 | tf_op jit(solution)/shard_map/ppermute | solution.py:20
  146.9 19.0 %multiply_subtract_fusion.3 = (f32[2,4,8,512]{3,2,1,0:T(8,128)S(1)}, f32[2,4,8,512]{3,2,1,0:T(8,128)S(1)}, f32[2,4,8,512]{3,2,1,0:T(8,128)S(1)}) fusion(f32[4,8,512]{2,1,0:T(8,128)S(1)} %get-tuple-element.922, f32[4,8,512]{2,1,0:T(8,128)S(1)} %get-tuple-element.921, f32[4]{0:T(128)S(1)} %get-tuple-element.410, f32[4]{0:T(128)S(1)} %get-tuple-element.409, ...), kind=kLoop, calls=%fused_computation.999 | loop fusion | flops 21757952 | bytes 2835456 | tf_op jit(solution)/shard_map/sub | solution.py:49
  166.0 72.3 %while.29 = (s32[]{:T(128)}, f32[1,4,8,1024]{3,2,1,0:T(8,128)S(1)}, f32[4,1,9,9]{0,3,2,1:T(8,128)S(1)}, f32[1,8,1024]{2,1,0:T(8,128)S(1)}, f32[1,4,8,1024]{3,2,1...) while((s32[]{:T(128)}, f32[1,4,8,1024]{3,2,1,0:T(8,128)S(1)}, ...), condition=%wide.region_4.5_spmd.clone.clone, body=%wide.region_3.4_spmd.clone.clone.sunk | while | flops 11239426 | bytes 7006565 | solution.py:132
  166.4 3.9 %collective-permute-start.3 = (f32[1,4,4,1024]{3,2,1,0:T(4,128)S(1)}, f32[1,4,4,1024]{3,2,1,0:T(4,128)S(1)}, u32[]{:S(2)}, u32[]{:S(2)}) collective-permute-start(f32[1,4,4,1024]{3,2,1,0:T(4,128)S(1)} %get-tuple-element.1525), channel_id=1, source_target_pairs={{0,4},{4,8},{8,12},{1,5},{5,9},{9,13},{2,6},{6,10},{10,14},{3,7},{... | collective-permute-start | bytes 196616 | tf_op jit(solution)/shard_map/while/body/eval_jaxpr/ppermute | solution.py:20
  172.2 4.3 %collective-permute-done.4 = f32[1,4,4,1024]{3,2,1,0:T(4,128)S(1)} collective-permute-done((f32[1,4,4,1024]{3,2,1,0:T(4,128)S(1)}, f32[1,4,4,1024]{3,2,1,0:T(4,128)S(1)}, u32[]{:S(2)}, u32[]{:S(2)}) %collective-permute-start.4) | collective-permute-done | bytes 65568 | tf_op jit(solution)/shard_map/while/body/eval_jaxpr/ppermute | solution.py:21
  176.6 3.7 %multiply_subtract_fusion.11 = f32[1,4,8,512]{3,2,1,0:T(8,128)S(1)} fusion(f32[1,4,8,512]{3,2,1,0:T(8,128)S(1)} %get-tuple-element.1523, f32[1,4,8,512]{3,2,1,0:T(8,128)S(1)} %get-tuple-element.1524, f32[1,4,12,1024]{3,2,1,0:T(8,128)S(1)} %get-tuple-element.1527, f32[1,4,12,1024]{3,2,1,0:T(8,128)S(1)} %get-tuple-element.1528, ...), kind=kLoop, calls=%fused_computation.510.clone.1 | loop fusion | flops 5292032 | bytes 1509920 | tf_op jit(solution)/shard_map/while/body/eval_jaxpr/sub | solution.py:76
  180.2 3.7 %multiply_add_fusion.21 = f32[1,4,8,512]{3,2,1,0:T(8,128)S(1)} fusion(f32[1,4,8,512]{3,2,1,0:T(8,128)S(1)} %get-tuple-element.1523, f32[1,4,8,512]{3,2,1,0:T(8,128)S(1)} %get-tuple-element.1524, f32[1,4,12,1024]{3,2,1,0:T(8,128)S(1)} %get-tuple-element.1527, f32[1,4,12,1024]{3,2,1,0:T(8,128)S(1)} %get-tuple-element.1528, ...), kind=kLoop, calls=%fused_computation.508.clone.1 | loop fusion | flops 5292032 | bytes 1509920 | tf_op jit(solution)/shard_map/while/body/eval_jaxpr/add | solution.py:77
  185.2 4.9 %collective-permute-done.5 = f32[1,4,8,1024]{3,2,1,0:T(8,128)S(1)} collective-permute-done((f32[1,4,8,1024]{3,2,1,0:T(8,128)S(1)}, f32[1,4,8,1024]{3,2,1,0:T(8,128)S(1)}, u32[]{:S(2)}, u32[]{:S(2)}) %collective-permute-start.5) | collective-permute-done | bytes 131104 | tf_op jit(solution)/shard_map/while/body/eval_jaxpr/ppermute | solution.py:29
  190.5 3.6 %collective-permute-start.3 = (f32[1,4,4,1024]{3,2,1,0:T(4,128)S(1)}, f32[1,4,4,1024]{3,2,1,0:T(4,128)S(1)}, u32[]{:S(2)}, u32[]{:S(2)}) collective-permute-start(f32[1,4,4,1024]{3,2,1,0:T(4,128)S(1)} %get-tuple-element.1525), channel_id=1, source_target_pairs={{0,4},{4,8},{8,12},{1,5},{5,9},{9,13},{2,6},{6,10},{10,14},{3,7},{... | collective-permute-start | bytes 196616 | tf_op jit(solution)/shard_map/while/body/eval_jaxpr/ppermute | solution.py:20
  196.0 4.3 %collective-permute-done.4 = f32[1,4,4,1024]{3,2,1,0:T(4,128)S(1)} collective-permute-done((f32[1,4,4,1024]{3,2,1,0:T(4,128)S(1)}, f32[1,4,4,1024]{3,2,1,0:T(4,128)S(1)}, u32[]{:S(2)}, u32[]{:S(2)}) %collective-permute-start.4) | collective-permute-done | bytes 65568 | tf_op jit(solution)/shard_map/while/body/eval_jaxpr/ppermute | solution.py:21
  200.4 3.7 %multiply_subtract_fusion.11 = f32[1,4,8,512]{3,2,1,0:T(8,128)S(1)} fusion(f32[1,4,8,512]{3,2,1,0:T(8,128)S(1)} %get-tuple-element.1523, f32[1,4,8,512]{3,2,1,0:T(8,128)S(1)} %get-tuple-element.1524, f32[1,4,12,1024]{3,2,1,0:T(8,128)S(1)} %get-tuple-element.1527, f32[1,4,12,1024]{3,2,1,0:T(8,128)S(1)} %get-tuple-element.1528, ...), kind=kLoop, calls=%fused_computation.510.clone.1 | loop fusion | flops 5292032 | bytes 1509920 | tf_op jit(solution)/shard_map/while/body/eval_jaxpr/sub | solution.py:76
  204.1 3.7 %multiply_add_fusion.21 = f32[1,4,8,512]{3,2,1,0:T(8,128)S(1)} fusion(f32[1,4,8,512]{3,2,1,0:T(8,128)S(1)} %get-tuple-element.1523, f32[1,4,8,512]{3,2,1,0:T(8,128)S(1)} %get-tuple-element.1524, f32[1,4,12,1024]{3,2,1,0:T(8,128)S(1)} %get-tuple-element.1527, f32[1,4,12,1024]{3,2,1,0:T(8,128)S(1)} %get-tuple-element.1528, ...), kind=kLoop, calls=%fused_computation.508.clone.1 | loop fusion | flops 5292032 | bytes 1509920 | tf_op jit(solution)/shard_map/while/body/eval_jaxpr/add | solution.py:77
  209.1 6.9 %collective-permute-done.5 = f32[1,4,8,1024]{3,2,1,0:T(8,128)S(1)} collective-permute-done((f32[1,4,8,1024]{3,2,1,0:T(8,128)S(1)}, f32[1,4,8,1024]{3,2,1,0:T(8,128)S(1)}, u32[]{:S(2)}, u32[]{:S(2)}) %collective-permute-start.5) | collective-permute-done | bytes 131104 | tf_op jit(solution)/shard_map/while/body/eval_jaxpr/ppermute | solution.py:29
  221.6 4.3 %collective-permute-done.4 = f32[1,4,4,1024]{3,2,1,0:T(4,128)S(1)} collective-permute-done((f32[1,4,4,1024]{3,2,1,0:T(4,128)S(1)}, f32[1,4,4,1024]{3,2,1,0:T(4,128)S(1)}, u32[]{:S(2)}, u32[]{:S(2)}) %collective-permute-start.4) | collective-permute-done | bytes 65568 | tf_op jit(solution)/shard_map/while/body/eval_jaxpr/ppermute | solution.py:21
  226.0 3.7 %multiply_subtract_fusion.11 = f32[1,4,8,512]{3,2,1,0:T(8,128)S(1)} fusion(f32[1,4,8,512]{3,2,1,0:T(8,128)S(1)} %get-tuple-element.1523, f32[1,4,8,512]{3,2,1,0:T(8,128)S(1)} %get-tuple-element.1524, f32[1,4,12,1024]{3,2,1,0:T(8,128)S(1)} %get-tuple-element.1527, f32[1,4,12,1024]{3,2,1,0:T(8,128)S(1)} %get-tuple-element.1528, ...), kind=kLoop, calls=%fused_computation.510.clone.1 | loop fusion | flops 5292032 | bytes 1509920 | tf_op jit(solution)/shard_map/while/body/eval_jaxpr/sub | solution.py:76
  229.7 3.7 %multiply_add_fusion.21 = f32[1,4,8,512]{3,2,1,0:T(8,128)S(1)} fusion(f32[1,4,8,512]{3,2,1,0:T(8,128)S(1)} %get-tuple-element.1523, f32[1,4,8,512]{3,2,1,0:T(8,128)S(1)} %get-tuple-element.1524, f32[1,4,12,1024]{3,2,1,0:T(8,128)S(1)} %get-tuple-element.1527, f32[1,4,12,1024]{3,2,1,0:T(8,128)S(1)} %get-tuple-element.1528, ...), kind=kLoop, calls=%fused_computation.508.clone.1 | loop fusion | flops 5292032 | bytes 1509920 | tf_op jit(solution)/shard_map/while/body/eval_jaxpr/add | solution.py:77
  234.7 3.6 %collective-permute-done.5 = f32[1,4,8,1024]{3,2,1,0:T(8,128)S(1)} collective-permute-done((f32[1,4,8,1024]{3,2,1,0:T(8,128)S(1)}, f32[1,4,8,1024]{3,2,1,0:T(8,128)S(1)}, u32[]{:S(2)}, u32[]{:S(2)}) %collective-permute-start.5) | collective-permute-done | bytes 131104 | tf_op jit(solution)/shard_map/while/body/eval_jaxpr/ppermute | solution.py:29
  242.9 4.0 %collective-permute-done.9 = f32[1,4,4,1024]{3,2,1,0:T(4,128)S(1)} collective-permute-done((f32[1,4,4,1024]{3,2,1,0:T(4,128)S(1)}, f32[1,4,4,1024]{3,2,1,0:T(4,128)S(1)}, u32[]{:S(2)}, u32[]{:S(2)}) %collective-permute-start.9) | collective-permute-done | bytes 65568 | tf_op jit(solution)/shard_map/ppermute | solution.py:21
  247.1 3.6 %multiply_subtract_fusion.5 = f32[1,4,8,512]{3,2,1,0:T(8,128)S(1)} fusion(f32[1,4,8,512]{3,2,1,0:T(8,128)S(1)} %get-tuple-element.831, f32[1,4,8,512]{3,2,1,0:T(8,128)S(1)} %get-tuple-element.830, f32[1,4,12,1024]{3,2,1,0:T(8,128)S(1)} %get-tuple-element.835, f32[1,4,12,1024]{3,2,1,0:T(8,128)S(1)} %get-tuple-element.834, ...), kind=kLoop, calls=%fused_computation.1022 | loop fusion | flops 5292032 | bytes 1509920 | tf_op jit(solution)/shard_map/sub | solution.py:76
  250.8 3.7 %multiply_add_fusion.13 = f32[1,4,8,512]{3,2,1,0:T(8,128)S(1)} fusion(f32[1,4,8,512]{3,2,1,0:T(8,128)S(1)} %get-tuple-element.831, f32[1,4,8,512]{3,2,1,0:T(8,128)S(1)} %get-tuple-element.830, f32[1,4,12,1024]{3,2,1,0:T(8,128)S(1)} %get-tuple-element.835, f32[1,4,12,1024]{3,2,1,0:T(8,128)S(1)} %get-tuple-element.834, ...), kind=kLoop, calls=%fused_computation.1020 | loop fusion | flops 5292032 | bytes 1509920 | tf_op jit(solution)/shard_map/add | solution.py:77
  254.5 9.1 %all_gather.12 = f32[4,4,8,1024]{3,2,1,0:T(8,128)S(1)} all-gather(f32[1,4,8,1024]{3,2,1,0:T(8,128)S(1)} %maximum_select_fusion.1), channel_id=1, replica_groups=mesh['shots'=2,'lat'=4,'depth'=4] {'depth'}, dimensions={0}, use_global_device_ids=true | all-gather | bytes 655360 | tf_op jit(solution)/shard_map/all_gather | solution.py:10
  (202 shorter events, 48.6 us)
Async XLA Ops:
  0.7 0.7 copy-start.7
  2.5 0.7 copy-start.5
  2.6 0.7 copy-start.6
  32.1 0.9 copy-start.1
  33.1 0.7 copy-start.4
  33.1 1.4 copy-start
  34.5 0.7 copy-start.2
  35.2 6.9 %collective-permute-start = (f32[2,4,4,1024]{3,2,1,0:T(4,128)S(1)}, f32[2,4,4,1024]{3,2,1,0:T(4,128)S(1)}, u32[]{:S(2)}, u32[]{:S(2)}) collective-permute-start(f32[2,4,4,1024]{3,2,1,0:T(4,128)S(1)} %get-tuple-element.1354), channel_id=1, source_target_pairs={{4,0},{8,4},{12,8},{5,1},{9,5},{13,9},{6,2},{10,6},{14,10},{7,3},{... | collective-permute-start | bytes 393224 | tf_op jit(solution)/shard_map/while/body/eval_jaxpr/ppermute | solution.py:21
  36.5 7.1 %collective-permute-start.1 = (f32[2,4,4,1024]{3,2,1,0:T(4,128)S(1)}, f32[2,4,4,1024]{3,2,1,0:T(4,128)S(1)}, u32[]{:S(2)}, u32[]{:S(2)}) collective-permute-start(f32[2,4,4,1024]{3,2,1,0:T(4,128)S(1)} %get-tuple-element.1445), channel_id=1, source_target_pairs={{0,4},{4,8},{8,12},{1,5},{5,9},{9,13},{2,6},{6,10},{10,14},{3,7},{... | collective-permute-start | bytes 393224 | tf_op jit(solution)/shard_map/while/body/eval_jaxpr/ppermute | solution.py:20
  62.8 2.4 collective-permute-start.2
  65.3 7.3 %collective-permute-start = (f32[2,4,4,1024]{3,2,1,0:T(4,128)S(1)}, f32[2,4,4,1024]{3,2,1,0:T(4,128)S(1)}, u32[]{:S(2)}, u32[]{:S(2)}) collective-permute-start(f32[2,4,4,1024]{3,2,1,0:T(4,128)S(1)} %get-tuple-element.1354), channel_id=1, source_target_pairs={{4,0},{8,4},{12,8},{5,1},{9,5},{13,9},{6,2},{10,6},{14,10},{7,3},{... | collective-permute-start | bytes 393224 | tf_op jit(solution)/shard_map/while/body/eval_jaxpr/ppermute | solution.py:21
  66.6 7.5 %collective-permute-start.1 = (f32[2,4,4,1024]{3,2,1,0:T(4,128)S(1)}, f32[2,4,4,1024]{3,2,1,0:T(4,128)S(1)}, u32[]{:S(2)}, u32[]{:S(2)}) collective-permute-start(f32[2,4,4,1024]{3,2,1,0:T(4,128)S(1)} %get-tuple-element.1445), channel_id=1, source_target_pairs={{0,4},{4,8},{8,12},{1,5},{5,9},{9,13},{2,6},{6,10},{10,14},{3,7},{... | collective-permute-start | bytes 393224 | tf_op jit(solution)/shard_map/while/body/eval_jaxpr/ppermute | solution.py:20
  93.3 6.6 %collective-permute-start.2 = (f32[2,4,8,1024]{3,2,1,0:T(8,128)S(1)}, f32[2,4,8,1024]{3,2,1,0:T(8,128)S(1)}, u32[]{:S(2)}, u32[]{:S(2)}) collective-permute-start(f32[2,4,8,1024]{3,2,1,0:T(8,128)S(1)} %pad_maximum_fusion.17), channel_id=1, source_target_pairs={{0,1},{1,2},{2,3},{4,5},{5,6},{6,7},{8,9},{9,10},{10,11},{12,13},{... | collective-permute-start | bytes 786440 | tf_op jit(solution)/shard_map/while/body/eval_jaxpr/ppermute | solution.py:29
  100.0 7.0 %collective-permute-start = (f32[2,4,4,1024]{3,2,1,0:T(4,128)S(1)}, f32[2,4,4,1024]{3,2,1,0:T(4,128)S(1)}, u32[]{:S(2)}, u32[]{:S(2)}) collective-permute-start(f32[2,4,4,1024]{3,2,1,0:T(4,128)S(1)} %get-tuple-element.1354), channel_id=1, source_target_pairs={{4,0},{8,4},{12,8},{5,1},{9,5},{13,9},{6,2},{10,6},{14,10},{7,3},{... | collective-permute-start | bytes 393224 | tf_op jit(solution)/shard_map/while/body/eval_jaxpr/ppermute | solution.py:21
  101.3 7.2 %collective-permute-start.1 = (f32[2,4,4,1024]{3,2,1,0:T(4,128)S(1)}, f32[2,4,4,1024]{3,2,1,0:T(4,128)S(1)}, u32[]{:S(2)}, u32[]{:S(2)}) collective-permute-start(f32[2,4,4,1024]{3,2,1,0:T(4,128)S(1)} %get-tuple-element.1445), channel_id=1, source_target_pairs={{0,4},{4,8},{8,12},{1,5},{5,9},{9,13},{2,6},{6,10},{10,14},{3,7},{... | collective-permute-start | bytes 393224 | tf_op jit(solution)/shard_map/while/body/eval_jaxpr/ppermute | solution.py:20
  127.7 8.0 %collective-permute-start.2 = (f32[2,4,8,1024]{3,2,1,0:T(8,128)S(1)}, f32[2,4,8,1024]{3,2,1,0:T(8,128)S(1)}, u32[]{:S(2)}, u32[]{:S(2)}) collective-permute-start(f32[2,4,8,1024]{3,2,1,0:T(8,128)S(1)} %pad_maximum_fusion.17), channel_id=1, source_target_pairs={{0,1},{1,2},{2,3},{4,5},{5,6},{6,7},{8,9},{9,10},{10,11},{12,13},{... | collective-permute-start | bytes 786440 | tf_op jit(solution)/shard_map/while/body/eval_jaxpr/ppermute | solution.py:29
  135.8 9.4 %collective-permute-start.6 = (f32[2,4,4,1024]{3,2,1,0:T(4,128)S(1)}, f32[2,4,4,1024]{3,2,1,0:T(4,128)S(1)}, u32[]{:S(2)}, u32[]{:S(2)}) collective-permute-start(f32[2,4,4,1024]{3,2,1,0:T(4,128)S(1)} %get-tuple-element.828), channel_id=1, source_target_pairs={{0,4},{4,8},{8,12},{1,5},{5,9},{9,13},{2,6},{6,10},{10,14},{3,7},{... | collective-permute-start | bytes 393224 | tf_op jit(solution)/shard_map/ppermute | solution.py:20
  139.8 6.9 %collective-permute-start.7 = (f32[2,4,4,1024]{3,2,1,0:T(4,128)S(1)}, f32[2,4,4,1024]{3,2,1,0:T(4,128)S(1)}, u32[]{:S(2)}, u32[]{:S(2)}) collective-permute-start(f32[2,4,4,1024]{3,2,1,0:T(4,128)S(1)} %get-tuple-element.829), channel_id=1, source_target_pairs={{4,0},{8,4},{12,8},{5,1},{9,5},{13,9},{6,2},{10,6},{14,10},{7,3},{... | collective-permute-start | bytes 393224 | tf_op jit(solution)/shard_map/ppermute | solution.py:21
  144.1 0.7 copy-start.3
  166.4 5.8 %collective-permute-start.3 = (f32[1,4,4,1024]{3,2,1,0:T(4,128)S(1)}, f32[1,4,4,1024]{3,2,1,0:T(4,128)S(1)}, u32[]{:S(2)}, u32[]{:S(2)}) collective-permute-start(f32[1,4,4,1024]{3,2,1,0:T(4,128)S(1)} %get-tuple-element.1525), channel_id=1, source_target_pairs={{0,4},{4,8},{8,12},{1,5},{5,9},{9,13},{2,6},{6,10},{10,14},{3,7},{... | collective-permute-start | bytes 196616 | tf_op jit(solution)/shard_map/while/body/eval_jaxpr/ppermute | solution.py:20
  170.3 6.2 %collective-permute-start.4 = (f32[1,4,4,1024]{3,2,1,0:T(4,128)S(1)}, f32[1,4,4,1024]{3,2,1,0:T(4,128)S(1)}, u32[]{:S(2)}, u32[]{:S(2)}) collective-permute-start(f32[1,4,4,1024]{3,2,1,0:T(4,128)S(1)} %get-tuple-element.1526), channel_id=1, source_target_pairs={{4,0},{8,4},{12,8},{5,1},{9,5},{13,9},{6,2},{10,6},{14,10},{7,3},{... | collective-permute-start | bytes 196616 | tf_op jit(solution)/shard_map/while/body/eval_jaxpr/ppermute | solution.py:21
  183.9 6.2 %collective-permute-start.5 = (f32[1,4,8,1024]{3,2,1,0:T(8,128)S(1)}, f32[1,4,8,1024]{3,2,1,0:T(8,128)S(1)}, u32[]{:S(2)}, u32[]{:S(2)}) collective-permute-start(f32[1,4,8,1024]{3,2,1,0:T(8,128)S(1)} %pad_maximum_fusion.19), channel_id=1, source_target_pairs={{1,0},{2,1},{3,2},{5,4},{6,5},{7,6},{9,8},{10,9},{11,10},{13,12},{... | collective-permute-start | bytes 393224 | tf_op jit(solution)/shard_map/while/body/eval_jaxpr/ppermute | solution.py:29
  190.5 5.5 %collective-permute-start.3 = (f32[1,4,4,1024]{3,2,1,0:T(4,128)S(1)}, f32[1,4,4,1024]{3,2,1,0:T(4,128)S(1)}, u32[]{:S(2)}, u32[]{:S(2)}) collective-permute-start(f32[1,4,4,1024]{3,2,1,0:T(4,128)S(1)} %get-tuple-element.1525), channel_id=1, source_target_pairs={{0,4},{4,8},{8,12},{1,5},{5,9},{9,13},{2,6},{6,10},{10,14},{3,7},{... | collective-permute-start | bytes 196616 | tf_op jit(solution)/shard_map/while/body/eval_jaxpr/ppermute | solution.py:20
  194.1 6.2 %collective-permute-start.4 = (f32[1,4,4,1024]{3,2,1,0:T(4,128)S(1)}, f32[1,4,4,1024]{3,2,1,0:T(4,128)S(1)}, u32[]{:S(2)}, u32[]{:S(2)}) collective-permute-start(f32[1,4,4,1024]{3,2,1,0:T(4,128)S(1)} %get-tuple-element.1526), channel_id=1, source_target_pairs={{4,0},{8,4},{12,8},{5,1},{9,5},{13,9},{6,2},{10,6},{14,10},{7,3},{... | collective-permute-start | bytes 196616 | tf_op jit(solution)/shard_map/while/body/eval_jaxpr/ppermute | solution.py:21
  207.8 8.2 %collective-permute-start.5 = (f32[1,4,8,1024]{3,2,1,0:T(8,128)S(1)}, f32[1,4,8,1024]{3,2,1,0:T(8,128)S(1)}, u32[]{:S(2)}, u32[]{:S(2)}) collective-permute-start(f32[1,4,8,1024]{3,2,1,0:T(8,128)S(1)} %pad_maximum_fusion.19), channel_id=1, source_target_pairs={{1,0},{2,1},{3,2},{5,4},{6,5},{7,6},{9,8},{10,9},{11,10},{13,12},{... | collective-permute-start | bytes 393224 | tf_op jit(solution)/shard_map/while/body/eval_jaxpr/ppermute | solution.py:29
  216.4 5.2 %collective-permute-start.3 = (f32[1,4,4,1024]{3,2,1,0:T(4,128)S(1)}, f32[1,4,4,1024]{3,2,1,0:T(4,128)S(1)}, u32[]{:S(2)}, u32[]{:S(2)}) collective-permute-start(f32[1,4,4,1024]{3,2,1,0:T(4,128)S(1)} %get-tuple-element.1525), channel_id=1, source_target_pairs={{0,4},{4,8},{8,12},{1,5},{5,9},{9,13},{2,6},{6,10},{10,14},{3,7},{... | collective-permute-start | bytes 196616 | tf_op jit(solution)/shard_map/while/body/eval_jaxpr/ppermute | solution.py:20
  219.7 6.2 %collective-permute-start.4 = (f32[1,4,4,1024]{3,2,1,0:T(4,128)S(1)}, f32[1,4,4,1024]{3,2,1,0:T(4,128)S(1)}, u32[]{:S(2)}, u32[]{:S(2)}) collective-permute-start(f32[1,4,4,1024]{3,2,1,0:T(4,128)S(1)} %get-tuple-element.1526), channel_id=1, source_target_pairs={{4,0},{8,4},{12,8},{5,1},{9,5},{13,9},{6,2},{10,6},{14,10},{7,3},{... | collective-permute-start | bytes 196616 | tf_op jit(solution)/shard_map/while/body/eval_jaxpr/ppermute | solution.py:21
  233.4 4.9 %collective-permute-start.5 = (f32[1,4,8,1024]{3,2,1,0:T(8,128)S(1)}, f32[1,4,8,1024]{3,2,1,0:T(8,128)S(1)}, u32[]{:S(2)}, u32[]{:S(2)}) collective-permute-start(f32[1,4,8,1024]{3,2,1,0:T(8,128)S(1)} %pad_maximum_fusion.19), channel_id=1, source_target_pairs={{1,0},{2,1},{3,2},{5,4},{6,5},{7,6},{9,8},{10,9},{11,10},{13,12},{... | collective-permute-start | bytes 393224 | tf_op jit(solution)/shard_map/while/body/eval_jaxpr/ppermute | solution.py:29
  238.6 4.3 %collective-permute-start.8 = (f32[1,4,4,1024]{3,2,1,0:T(4,128)S(1)}, f32[1,4,4,1024]{3,2,1,0:T(4,128)S(1)}, u32[]{:S(2)}, u32[]{:S(2)}) collective-permute-start(f32[1,4,4,1024]{3,2,1,0:T(4,128)S(1)} %get-tuple-element.836), channel_id=1, source_target_pairs={{0,4},{4,8},{8,12},{1,5},{5,9},{9,13},{2,6},{6,10},{10,14},{3,7},{... | collective-permute-start | bytes 196616 | tf_op jit(solution)/shard_map/ppermute | solution.py:20
  240.8 6.2 %collective-permute-start.9 = (f32[1,4,4,1024]{3,2,1,0:T(4,128)S(1)}, f32[1,4,4,1024]{3,2,1,0:T(4,128)S(1)}, u32[]{:S(2)}, u32[]{:S(2)}) collective-permute-start(f32[1,4,4,1024]{3,2,1,0:T(4,128)S(1)} %get-tuple-element.837), channel_id=1, source_target_pairs={{4,0},{8,4},{12,8},{5,1},{9,5},{13,9},{6,2},{10,6},{14,10},{7,3},{... | collective-permute-start | bytes 196616 | tf_op jit(solution)/shard_map/ppermute | solution.py:21
